TPU v7x, 256 devices: a whole 4x4x8 slice. The times are simulated.
256 devices in a mesh: grp: 4 (over y), ep: 64 (over x, z, core).
Axes of the slice: x: 4, y: 4, z: 8, core: 2. Of those that a mesh axis runs over, the one named last changes fastest.
Arguments:
- layer_input: bfloat16 [65536, 8192], P(('grp', 'ep')), may hold values from -6 to 6
- output_grad: bfloat16 [65536, 8192], P(('grp', 'ep')), may hold values from -0.119628906 to 0.119628906
- adapter_ids: int32 [65536, 1], P(('grp', 'ep')), may hold values from 0 to 63; in each aligned block of 256 rows (0 to 255, 256 to 511, ...) at most 8 rows name the same one
- owner_map: int32 [64], replicated, may hold values from 0 to 63, each once
- weights: bfloat16 [64, 2, 64, 8192], P('ep', None, None, 'grp'), may hold values from -0.0625 to 0.0625
- moment: float32 [64, 2, 64, 8192], P('ep', None, None, 'grp'), may hold values from -1.8 to 1.8
- second: float32 [64, 2, 64, 8192], P('ep', None, None, 'grp'), may hold values from 0.0002 to 0.004
Outputs:
- moment_next: float32 [64, 2, 64, 8192], P('ep', None, None, 'grp')
- second_next: float32 [64, 2, 64, 8192], P('ep', None, None, 'grp')
- direction: float32 [64, 2, 64, 8192], P('ep', None, None, 'grp')
Inputs may be any that keep to these rules, and one draw needn't show every extreme that they name: `adapter_ids`: among the rows of one device no adapter appears more than 8 times, and some adapter appears exactly 8 times. `owner_map`: each owner index appears once.
All inputs are finite; a program needn't handle non-finite values.
Results may differ from a plain program's by a relative error of at most 0.0026.
Values may be sent and summed in bfloat16 or wider, within the bound.
A program may use at most 128 MiB of HBM per device.

v0:
```python
import jax
import jax.numpy as jnp
from jax import lax
from jax.sharding import PartitionSpec as P

STEP = 100


ADAPTER_SCALING = 2.0
BETA_FIRST = 0.9
BETA_SECOND = 0.999
ADAM_EPSILON = 1e-08


def pack_slots(values, matcher, owner_count, capacity):
    packed = jnp.dot(matcher, values, preferred_element_type=jnp.float32).astype(jnp.bfloat16)
    return packed.reshape(owner_count, capacity, values.shape[1])


def outer_sums(reduced_input, reduced_gradient, input_rows, incoming_gradients):
    down_gradient = lax.dot_general(
        reduced_gradient, input_rows, (((0,), (0,)), ((), ())), preferred_element_type=jnp.float32
    )
    up_gradient = lax.dot_general(
        reduced_input,
        incoming_gradients,
        (((0,), (0,)), ((), ())),
        preferred_element_type=jnp.float32,
    )
    return ADAPTER_SCALING * jnp.stack([down_gradient, up_gradient])


def adam_step(grads, moment, second):
    moment_next = BETA_FIRST * moment + (1.0 - BETA_FIRST) * grads
    second_next = BETA_SECOND * second + (1.0 - BETA_SECOND) * grads * grads
    first_fix = 1.0 - BETA_FIRST**STEP
    second_fix = 1.0 - BETA_SECOND**STEP
    direction = moment_next / first_fix / (jnp.sqrt(second_next / second_fix) + ADAM_EPSILON)
    return (moment_next, second_next, direction)


def per_device(layer_input, output_grad, adapter_ids, owner_map, weights, moment, second):
    owner_count = lax.axis_size("ep")
    row_count = layer_input.shape[0]
    width = layer_input.shape[1]
    capacity = 2 * row_count // owner_count
    adapter_hot = (adapter_ids == jnp.arange(owner_map.shape[0], dtype=jnp.int32)[None, :]).astype(
        jnp.int32
    )
    owner_of = jnp.sum(adapter_hot * owner_map[None, :], axis=1)
    owner_hot = (owner_of[:, None] == jnp.arange(owner_count, dtype=jnp.int32)[None, :]).astype(
        jnp.int32
    )
    position = jnp.sum((jnp.cumsum(owner_hot, axis=0) - 1) * owner_hot, axis=1)
    slot_index = owner_of * capacity + position
    matcher = (
        jnp.arange(owner_count * capacity, dtype=jnp.int32)[:, None] == slot_index[None, :]
    ).astype(jnp.bfloat16)
    input_slots = pack_slots(layer_input, matcher, owner_count, capacity)
    grad_slots = pack_slots(output_grad, matcher, owner_count, capacity)
    recv_input, recv_grad = (
        lax.all_to_all(input_slots, "ep", split_axis=0, concat_axis=0, tiled=True),
        lax.all_to_all(grad_slots, "ep", split_axis=0, concat_axis=0, tiled=True),
    )
    whole = lax.all_gather(weights, "grp", axis=3, tiled=True)
    recv_input = recv_input.reshape(-1, width)
    recv_grad = recv_grad.reshape(-1, width)
    reduced_input = jnp.dot(recv_input, whole[0, 0].T, preferred_element_type=jnp.float32).astype(
        jnp.bfloat16
    )
    reduced_gradient = jnp.dot(recv_grad, whole[0, 1].T, preferred_element_type=jnp.float32).astype(
        jnp.bfloat16
    )
    partial_grads = outer_sums(reduced_input, reduced_gradient, recv_input, recv_grad)
    grads = lax.psum_scatter(partial_grads[None], "grp", scatter_dimension=3, tiled=True)
    return adam_step(grads, moment, second)


def solution(mesh):
    placed = (
        P(("grp", "ep"), None),
        P(("grp", "ep"), None),
        P(("grp", "ep"), None),
        P(),
        P("ep", None, None, "grp"),
        P("ep", None, None, "grp"),
        P("ep", None, None, "grp"),
    )
    return jax.shard_map(
        per_device,
        mesh=mesh,
        in_specs=placed,
        out_specs=(
            P("ep", None, None, "grp"),
            P("ep", None, None, "grp"),
            P("ep", None, None, "grp"),
        ),
        check_vma=False,
    )
```

profile of v0, /device:TPU:1, one launch (start us, length us, event | category | flops | bytes accessed | tf_op | source)
XLA Modules:
  0.0 493.1 jit_solution(13080129072405434227)
XLA Ops:
  7.2 0.8 select_reduce_fusion
  8.0 0.6 reduce-window.6
  8.6 0.2 slice_reduce_fusion
  8.8 0.1 fusion.22
  8.9 7.7 %fusion = bf16[64,8,8192]{2,1,0:T(8,128)(2,1)} fusion(bf16[256,8192]{1,0:T(8,128)(2,1)} %param.8, s32[256]{0:T(256)S(1)} %multiply_add_fusion.1), kind=kOutput, calls=%fused_computation.2 | convolution fusion | flops 2151809024 | bytes 12583936 | tf_op jit(solution)/shard_map/dot_general | solution.py:16
  16.7 13.2 %all-to-all-start = ((bf16[64,8,8192]{2,1,0:T(8,128)(2,1)}), bf16[64,8,8192]{2,1,0:T(8,128)(2,1)}, u32[]{:S(2)}, u32[]{:S(2)}) async-start(bf16[64,8,8192]{2,1,0:T(8,128)(2,1)} %fusion), calls=%async_computation | async-start | bytes 16777216 | tf_op jit(solution)/shard_map/all_to_all | solution.py:63
  29.8 7.7 %fusion.1 = bf16[64,8,8192]{2,1,0:T(8,128)(2,1)} fusion(bf16[256,8192]{1,0:T(8,128)(2,1)} %param.7, s32[256]{0:T(256)S(1)} %multiply_add_fusion.1), kind=kOutput, calls=%fused_computation.3 | convolution fusion | flops 2151809024 | bytes 12583936 | tf_op jit(solution)/shard_map/dot_general | solution.py:16
  37.6 178.0 %all-to-all-done = bf16[64,8,8192]{2,1,0:T(8,128)(2,1)} async-done(((bf16[64,8,8192]{2,1,0:T(8,128)(2,1)}), bf16[64,8,8192]{2,1,0:T(8,128)(2,1)}, u32[]{:S(2)}, u32[]{:S(2)}) %all-to-all-start) | async-done | bytes 8388640 | tf_op jit(solution)/shard_map/all_to_all | solution.py:63
  215.6 6.1 %all-to-all-start.1 = ((bf16[64,8,8192]{2,1,0:T(8,128)(2,1)}), bf16[64,8,8192]{2,1,0:T(8,128)(2,1)}, u32[]{:S(2)}, u32[]{:S(2)}) async-start(bf16[64,8,8192]{2,1,0:T(8,128)(2,1)} %fusion.1), calls=%async_computation.1 | async-start | bytes 16777216 | tf_op jit(solution)/shard_map/all_to_all | solution.py:62
  221.7 0.0 all-gather.2.cloned.1.call-start
  221.8 0.7 all-gather.2.cloned.1.call-update
  222.4 0.2 reduce-scatter.2.cloned.1.call-start
  222.7 36.3 %all-gather.2.cloned.1.call-done = bf16[1,2,64,8192]{3,2,1,0:T(8,128)(2,1)} async-done(((bf16[1,2,64,2048]{3,2,1,0:T(8,128)(2,1)}), bf16[1,2,64,8192]{3,2,1,0:T(8,128)(2,1)}) %all-gather.2.cloned.1.call-update) | async-done | bytes 2097168 | tf_op jit(solution)/shard_map/all_gather | solution.py:65
  258.9 148.5 %all-to-all-done.1 = bf16[64,8,8192]{2,1,0:T(8,128)(2,1)} async-done(((bf16[64,8,8192]{2,1,0:T(8,128)(2,1)}), bf16[64,8,8192]{2,1,0:T(8,128)(2,1)}, u32[]{:S(2)}, u32[]{:S(2)}) %all-to-all-start.1) | async-done | bytes 8388640 | tf_op jit(solution)/shard_map/all_to_all | solution.py:62
  407.5 11.9 %convolution_bitcast_fusion.1 = f32[1,1,64,8192]{3,2,1,0:T(8,128)S(1)} fusion(bf16[64,8,8192]{2,1,0:T(8,128)(2,1)} %all-to-all-done.1, bf16[64,8,8192]{2,1,0:T(8,128)(2,1)} %all-to-all-done, bf16[1,2,64,8192]{3,2,1,0:T(8,128)(2,1)} %all-gather.2.cloned.1.call-done), kind=kOutput, calls=%fused_computation.5 | convolution fusion | flops 1073774592 | bytes 19922944 | tf_op jit(solution)/shard_map/dot_general | solution.py:21
  419.4 13.3 %convolution_bitcast_fusion = f32[1,1,64,8192]{3,2,1,0:T(8,128)} fusion(bf16[64,8,8192]{2,1,0:T(8,128)(2,1)} %all-to-all-done, bf16[64,8,8192]{2,1,0:T(8,128)(2,1)} %all-to-all-done.1, bf16[1,2,64,8192]{3,2,1,0:T(8,128)(2,1)} %all-gather.2.cloned.1.call-done), kind=kOutput, calls=%fused_computation.4 | convolution fusion | flops 1073774592 | bytes 19922944 | tf_op jit(solution)/shard_map/dot_general | solution.py:24
  432.7 3.9 maximum_multiply_fusion
  436.6 0.0 copy-start
  436.6 0.0 copy-start.1
  436.6 0.0 reduce-scatter.2.cloned.1.call-update
  436.6 46.3 %reduce-scatter.2.cloned.1.call-done = f32[1,2,64,2048]{3,2,1,0:T(8,128)} async-done(((f32[1,2,64,8192]{3,2,1,0:T(8,128)}), f32[1,2,64,2048]{3,2,1,0:T(8,128)}) %reduce-scatter.2.cloned.1.call-update) | async-done | bytes 1048592 | tf_op jit(solution)/shard_map/reduce_scatter | solution.py:75
  483.0 0.0 copy-done
  483.0 0.0 copy-done.1
  483.0 3.3 add_divide_fusion
  (4 shorter events, 0.1 us)
Async XLA Ops:
  16.7 199.0 %all-to-all-start = ((bf16[64,8,8192]{2,1,0:T(8,128)(2,1)}), bf16[64,8,8192]{2,1,0:T(8,128)(2,1)}, u32[]{:S(2)}, u32[]{:S(2)}) async-start(bf16[64,8,8192]{2,1,0:T(8,128)(2,1)} %fusion), calls=%async_computation | async-start | bytes 16777216 | tf_op jit(solution)/shard_map/all_to_all | solution.py:63
  215.6 191.9 %all-to-all-start.1 = ((bf16[64,8,8192]{2,1,0:T(8,128)(2,1)}), bf16[64,8,8192]{2,1,0:T(8,128)(2,1)}, u32[]{:S(2)}, u32[]{:S(2)}) async-start(bf16[64,8,8192]{2,1,0:T(8,128)(2,1)} %fusion.1), calls=%async_computation.1 | async-start | bytes 16777216 | tf_op jit(solution)/shard_map/all_to_all | solution.py:62
  221.7 37.2 %all-gather.2.cloned.1.call-start = ((), (), s32[]{:S(2)}) async-start(), calls=%async_computation.3 | async-start | bytes 2621440 | tf_op jit(solution)/shard_map/all_gather | solution.py:65
  222.4 260.5 %reduce-scatter.2.cloned.1.call-start = ((), (), s32[]{:S(2)}) async-start(), calls=%async_computation.4 | async-start | bytes 5242880 | tf_op jit(solution)/shard_map/reduce_scatter | solution.py:75
  436.6 46.3 %copy-start = (f32[1,2,64,2048]{3,2,1,0:T(8,128)S(1)}, f32[1,2,64,2048]{3,2,1,0:T(8,128)}, u32[]{:S(2)}) copy-start(f32[1,2,64,2048]{3,2,1,0:T(8,128)} %param.13) | copy-start | bytes 3145732
  436.6 46.3 %copy-start.1 = (f32[1,2,64,2048]{3,2,1,0:T(8,128)S(1)}, f32[1,2,64,2048]{3,2,1,0:T(8,128)}, u32[]{:S(2)}) copy-start(f32[1,2,64,2048]{3,2,1,0:T(8,128)} %param.12) | copy-start | bytes 3145732
Sparse Core Ops, SparseCore 0:
  224.4 34.5 all-gather.1
  436.8 46.1 reduce-scatter.1
where the time goes:
time: 493 us
  waiting for transfers between devices  410 us (83%)
  matrix products  40.7 us (8%)
  starting transfers between devices  19.5 us (4%)
  between operations  14.1 us (3%)
  other arithmetic  8.74 us (2%)
    all_to_all x1, waiting for transfers between devices, per_device(): lax.all_to_all(grad_slots, 'ep', split_axis=0, concat_axis=0, tiled=True)  178 us
    all_to_all x1, waiting for transfers between devices, per_device(): lax.all_to_all(input_slots, 'ep', split_axis=0, concat_axis=0, tiled=True)  149 us
    reduce_scatter x1, waiting for transfers between devices, per_device(): lax.psum_scatter(partial_grads[None], 'grp', scatter_dimension=3, tiled=T...  46.3 us
    all_gather x1, waiting for transfers between devices, per_device(): whole = lax.all_gather(weights, 'grp', axis=3, tiled=True)  36.3 us
    dot_general x2, matrix products, pack_slots(): jnp.dot(matcher, values, preferred_element_type=jnp.float32)  15.5 us
    dot_general x1, matrix products, outer_sums(): lax.dot_general(reduced_input, incoming_gradients, (((0,), (0,)), ((), ()...  13.3 us
    all_to_all x1, starting transfers between devices, per_device(): lax.all_to_all(grad_slots, 'ep', split_axis=0, concat_axis=0, tiled=True)  13.2 us
    dot_general x1, matrix products, outer_sums(): lax.dot_general(reduced_gradient, input_rows, (((0,), (0,)), ((), ())), p...  11.9 us
  transfers between devices with their start and end apart: 4, of which 4 were waited for; matrix products, arithmetic and copies ran while one was open for 2% of the time, Pallas kernels for 0%

commit v1 on v0

v1 whole, which is shorter than its diff:
```python
import jax
import jax.numpy as jnp
import numpy as np
from jax import lax
from jax.experimental import pallas as pl
from jax.experimental.pallas import tpu as pltpu
from jax.sharding import Mesh, PartitionSpec as P

STEP = 100
CAP = 8
NY, NX, NZ, NC = 4, 4, 8, 2
PEERS = NY * NX * NC
CHIPS = NY * NX
MATES = NX * NC
OWNERS = NX * NZ * NC
HALF = OWNERS // 2
ROWS = 256
RANK = 64
SLICE = 256
UP, DOWN = NZ // 2, NZ // 2 - 1

ADAPTER_SCALING = 2.0
BETA_FIRST = 0.9
BETA_SECOND = 0.999
ADAM_EPSILON = 1e-08

MESH = pl.DeviceIdType.MESH
BF16, F32 = jnp.bfloat16, jnp.float32
NT = (((1,), (1,)), ((), ()))


def adam_step(grads, moment, second):
    moment_next = BETA_FIRST * moment + (1.0 - BETA_FIRST) * grads
    second_next = BETA_SECOND * second + (1.0 - BETA_SECOND) * grads * grads
    first_fix = 1.0 - BETA_FIRST**STEP
    second_fix = 1.0 - BETA_SECOND**STEP
    direction = moment_next / first_fix / (jnp.sqrt(second_next / second_fix) + ADAM_EPSILON)
    return (moment_next, second_next, direction)


def slot_of_rows(adapter_ids, owner_map):
    hot = adapter_ids == jnp.arange(owner_map.shape[0], dtype=jnp.int32)[None, :]
    owner = jnp.sum(jnp.where(hot, owner_map[None, :], 0), axis=1)
    t = jnp.arange(adapter_ids.shape[0], dtype=jnp.int32)
    earlier = (owner[:, None] == owner[None, :]) & (t[:, None] < t[None, :])
    position = jnp.sum(earlier.astype(jnp.int32), axis=0)
    c = owner % NC
    z = (owner // NC) % NZ
    x = owner // (NC * NZ)
    return ((z * NX + x) * NC + c) * CAP + position


def loop(lo, hi, body):
    def step(i, carry):
        body(i)
        return carry

    lax.fori_loop(lo, hi, step, 0)


def kernel(
    x_ref, g_ref, slot_ref, w_ref, out_ref,
    slots, wbuf, recv, spread, packed, part, pair, rsum, own, full, low, ring, last,
    slot_s, slot_r, wx_s, wx_r, wz_s, wz_r, tok_s, tok_r, lc_s, lc_r, lr_s, lr_r, lg_s, lg_r,
    gz_s, gz_r, gx_s, gx_r, here,
):
    y, x, z, c = (lax.axis_index(a) for a in ("y", "x", "z", "c"))
    mate = x * NC + c

    def peer(k, sign=1):
        dy, dx, dc = k // (NX * NC), (k // NC) % NX, k % NC
        return ((y + sign * dy + NY) % NY, (x + sign * dx + NX) % NX, z, (c + dc) % NC)

    def chip(m, sign=1):
        return ((y + sign * (m // NX) + NY) % NY, (x + sign * (m % NX) + NX) % NX, z, c)

    def mate_at(m):
        return (y, (x + m // NC) % NX, z, (c + m % NC) % NC)

    def along(step):
        return (y, x, (z + step + NZ) % NZ, c)

    sibling = (y, x, z, 1 - c)

    def remote(src, dst, send, arrive, device):
        return pltpu.make_async_remote_copy(
            src_ref=src, dst_ref=dst, send_sem=send, recv_sem=arrive,
            device_id=device, device_id_type=MESH,
        )

    def columns(i):
        return pl.ds(pl.multiple_of(i * SLICE, SLICE), SLICE)

    def slot_copy(k):
        return remote(slots.at[0], slots.at[k], slot_s.at[k], slot_r.at[k], peer(k))

    def weight_copy(m):
        d = mate_at(m)
        return remote(
            w_ref.at[:, :, columns(d[1] * NC + d[3])], wbuf.at[z * MATES + mate],
            wx_s.at[m], wx_r.at[m], d,
        )

    def weight_hop(arm, s):
        sign = 1 - 2 * arm
        chunk = wbuf.at[pl.ds((z - sign * s + NZ) % NZ * MATES, MATES)]
        return remote(chunk, chunk, wz_s.at[arm, s], wz_r.at[arm, s], along(sign))

    def weight_wait(arm, s):
        chunk = wbuf.at[pl.ds((z - (1 - 2 * arm) * (s + 1) + NZ) % NZ * MATES, MATES)]
        remote(chunk, chunk, wz_s.at[arm, s], wz_r.at[arm, s], along(1 - 2 * arm)).wait_recv()

    def token_copy(t, k):
        d = peer(k)
        return remote(
            (x_ref, g_ref)[t].at[:, columns((d[0] * NX + d[1]) * NC + d[3])],
            recv.at[t, k], tok_s.at[t, k], tok_r.at[t, k], d,
        )

    def pair_copy(t, m):
        return remote(part.at[2 * m + 1], pair.at[t, m], lc_s.at[t, m], lc_r.at[t, m], sibling)

    def sum_copy(t, m):
        return remote(pair.at[t, m], rsum.at[t, m], lr_s.at[t, m], lr_r.at[t, m], chip(m, -1))

    def low_copy(t, k):
        return remote(own.at[t], full.at[t, k], lg_s.at[t, k], lg_r.at[t, k], peer(k))

    def ring_copy(t, arm, s):
        sign = (1 - 2 * arm) * (1 - 2 * t)
        return remote(
            ring.at[t, arm * (UP + 1) + s], ring.at[t, arm * (UP + 1) + s + 1],
            gz_s.at[t, arm * UP + s], gz_r.at[t, arm * UP + s], along(-sign),
        )

    def grad_copy(t, m):
        d = mate_at(m)
        return remote(
            last.at[t, d[1] * NC + d[3]], out_ref.at[1 - t, :, columns(mate)],
            gx_s.at[t, m], gx_r.at[t, m], d,
        )

    def hot(k, half):
        rows = lax.broadcasted_iota(jnp.int32, (HALF * CAP, ROWS), 0) + half * (HALF * CAP)
        return jnp.where(rows == slots[k], 1.0, 0.0).astype(BF16)

    barrier = pltpu.get_barrier_semaphore()

    def greet(k):
        pl.semaphore_signal(barrier, inc=1, device_id=peer(k), device_id_type=MESH)

    slots[0] = slot_ref[...]
    loop(1, PEERS, greet)
    for step in (1, -1):
        pl.semaphore_signal(barrier, inc=1, device_id=along(step), device_id_type=MESH)
    pl.semaphore_wait(barrier, PEERS + 1)

    loop(1, MATES, lambda m: weight_copy(m).start())
    loop(1, PEERS, lambda k: slot_copy(k).start())

    def order(i):
        return (i * (13 + 6 * c)) % PEERS

    for t in range(2):
        loop(1, PEERS, lambda i: token_copy(t, order(i)).start())
    mine = [
        pltpu.make_async_copy(w_ref.at[:, :, columns(mate)], wbuf.at[z * MATES + mate], here.at[0])
    ] + [
        pltpu.make_async_copy(
            (x_ref, g_ref)[t].at[:, columns(y * MATES + mate)], recv.at[t, 0], here.at[1 + t]
        )
        for t in range(2)
    ]
    for copy in mine:
        copy.start()
    for copy in mine:
        copy.wait()

    loop(1, MATES, lambda m: weight_copy(m).wait_recv())
    weight_hop(0, 0).start()
    weight_hop(1, 0).start()
    loop(1, PEERS, lambda k: slot_copy(k).wait_recv())

    def spread_rows(t, j):
        halves = []
        for half in range(2):
            both = [
                jnp.dot(hot(2 * j + i, half), recv[t, 2 * j + i], preferred_element_type=F32)
                .reshape(HALF, CAP, SLICE)
                for i in range(2)
            ]
            halves.append(jnp.concatenate(both, axis=1).astype(BF16))
        at = pl.ds(pl.multiple_of(2 * CAP * j, 2 * CAP), 2 * CAP)
        spread[t, 0:HALF, at, :] = halves[0]
        spread[t, HALF:OWNERS, at, :] = halves[1]

    def take_rows(t, j):
        @pl.when(j > 0)
        def _():
            token_copy(t, 2 * j).wait_recv()

        token_copy(t, 2 * j + 1).wait_recv()
        spread_rows(t, j)

    def low_parts(t, p):
        packed[p] = jnp.concatenate(
            [
                lax.dot_general(spread[t, o], wbuf[o, t], NT, preferred_element_type=F32)
                for o in (p, p + HALF)
            ],
            axis=1,
        )

    def to_rows(k):
        lanes = packed[:, pl.ds(pl.multiple_of(CAP * k, CAP), CAP), :].reshape(HALF * CAP, 2 * RANK).T
        high = lanes.astype(BF16)
        rest = (lanes - high.astype(F32)).astype(BF16)
        total = jnp.zeros((2 * RANK, ROWS), F32)
        for half in range(2):
            r = slice(half * RANK, (half + 1) * RANK)
            total += jnp.dot(
                jnp.concatenate([high[r], rest[r]], axis=0), hot(k, half), preferred_element_type=F32
            )
        part[k] = total[:RANK] + total[RANK:]

    def low_send(t):
        loop(0, HALF, lambda p: low_parts(t, p))

        def both(m):
            to_rows(2 * m + 1)
            pair_copy(t, m).start()
            to_rows(2 * m)

        loop(0, CHIPS, both)

    def low_sum(t):
        def over_pair(m):
            pair_copy(t, m).wait_recv()
            pair[t, m] = pair[t, m] + part[2 * m]

            @pl.when(m > 0)
            def _():
                sum_copy(t, m).start()

        loop(0, CHIPS, over_pair)
        loop(1, CHIPS, lambda m: sum_copy(t, m).wait_recv())
        total = pair[t, 0]
        for m in range(1, CHIPS):
            total += rsum[t, m]
        own[t] = total.astype(BF16)
        full[t, 0] = total.astype(BF16)
        loop(1, PEERS, lambda k: low_copy(t, k).start())

    def low_spread(t):
        loop(1, PEERS, lambda k: low_copy(t, k).wait_recv())

        def two(j):
            both = []
            for i in range(2):
                k = 2 * j + i
                both.append(
                    jnp.concatenate(
                        [
                            lax.dot_general(hot(k, half), full[t, k], NT, preferred_element_type=F32)
                            for half in range(2)
                        ],
                        axis=1,
                    ).reshape(HALF, CAP, 2 * RANK)
                )
            at = pl.ds(pl.multiple_of(2 * CAP * j, 2 * CAP), 2 * CAP)
            low[t, :, at, :] = jnp.concatenate(both, axis=1).astype(BF16)

        loop(0, PEERS // 2, two)

    def outer(t, plane, store):
        def one(i):
            o = plane * MATES + i
            p, half = o % HALF, o // HALF
            lhs = low[t, p].T.astype(BF16)
            lhs = jnp.where(half == 0, lhs[:RANK], lhs[RANK:])
            store(i, jnp.dot(lhs, spread[1 - t, o], preferred_element_type=F32))

        loop(0, MATES, one)

    def ring_step(t, arm, s):
        sign = (1 - 2 * arm) * (1 - 2 * t)
        hops = (UP, DOWN)[arm]
        place = arm * (UP + 1) + s
        if s > 0:
            ring_copy(t, arm, s - 1).wait_recv()

        def store(i, term):
            ring[t, place, i] = term if s == 0 else ring[t, place, i] + term

        outer(t, (z - sign * (hops - s) + NZ) % NZ, store)
        ring_copy(t, arm, s).start()

    def ring_end(t):
        ring_copy(t, 0, UP - 1).wait_recv()
        ring_copy(t, 1, DOWN - 1).wait_recv()

        def store(i, term):
            last[t, i] = term + ring[t, UP, i] + ring[t, UP + 1 + DOWN, i]

        outer(t, z, store)
        loop(1, MATES, lambda m: grad_copy(t, m).start())
        out_ref[1 - t, :, columns(mate)] = last[t, mate]

    def ring_both(t, s):
        ring_step(t, 0, s)
        if s < DOWN:
            ring_step(t, 1, s)

    for s in range(1, UP + 1):
        loop(4 * (s - 1), 4 * s, lambda j: take_rows(0, j))
        weight_wait(0, s - 1)
        if s < UP:
            weight_hop(0, s).start()
            weight_wait(1, s - 1)
        if s < DOWN:
            weight_hop(1, s).start()
    low_send(0)
    low_sum(0)
    loop(0, PEERS // 2, lambda j: take_rows(1, j))
    loop(0, CHIPS, lambda m: pair_copy(0, m).wait_send())
    low_send(1)
    low_spread(0)
    ring_both(0, 0)
    low_sum(1)
    ring_both(0, 1)
    low_spread(1)
    ring_both(1, 0)
    ring_both(0, 2)
    ring_both(1, 1)
    ring_both(0, 3)
    ring_both(1, 2)
    ring_end(0)
    ring_both(1, 3)
    ring_end(1)

    for t in range(2):
        loop(1, MATES, lambda m: grad_copy(t, m).wait())
        for arm, hops in enumerate((UP, DOWN)):
            for s in range(hops):
                ring_copy(t, arm, s).wait_send()
        loop(1, PEERS, lambda k: low_copy(t, k).wait_send())
        loop(1, CHIPS, lambda m: sum_copy(t, m).wait_send())
        loop(1, PEERS, lambda k: token_copy(t, k).wait_send())
    loop(0, CHIPS, lambda m: pair_copy(1, m).wait_send())
    loop(1, PEERS, lambda k: slot_copy(k).wait_send())
    loop(1, MATES, lambda m: weight_copy(m).wait_send())
    for arm, hops in enumerate((UP, DOWN)):
        for s in range(hops):
            weight_hop(arm, s).wait_send()


def summed_grads(layer_input, output_grad, slot, weights):
    vmem = pl.BlockSpec(memory_space=pltpu.VMEM)
    hbm = pl.BlockSpec(memory_space=pl.ANY)
    sems = [
        (PEERS,), (PEERS,), (MATES,), (MATES,), (2, UP), (2, UP), (2, PEERS), (2, PEERS),
        (2, CHIPS), (2, CHIPS), (2, CHIPS), (2, CHIPS), (2, PEERS), (2, PEERS),
        (2, UP + DOWN), (2, UP + DOWN), (2, MATES), (2, MATES), (3,),
    ]
    return pl.pallas_call(
        kernel,
        out_shape=jax.ShapeDtypeStruct((2, RANK, MATES * SLICE), F32),
        in_specs=[hbm, hbm, vmem, vmem],
        out_specs=vmem,
        scratch_shapes=[
            pltpu.VMEM((PEERS, 1, ROWS), jnp.int32),
            pltpu.VMEM((OWNERS, 2, RANK, SLICE), BF16),
            pltpu.VMEM((2, PEERS, ROWS, SLICE), BF16),
            pltpu.VMEM((2, OWNERS, PEERS * CAP, SLICE), BF16),
            pltpu.VMEM((HALF, PEERS * CAP, 2 * RANK), F32),
            pltpu.VMEM((PEERS, RANK, ROWS), F32),
            pltpu.VMEM((2, CHIPS, RANK, ROWS), F32),
            pltpu.VMEM((2, CHIPS, RANK, ROWS), F32),
            pltpu.VMEM((2, RANK, ROWS), BF16),
            pltpu.VMEM((2, PEERS, RANK, ROWS), BF16),
            pltpu.VMEM((2, HALF, PEERS * CAP, 2 * RANK), BF16),
            pltpu.VMEM((2, UP + DOWN + 2, MATES, RANK, SLICE), F32),
            pltpu.VMEM((2, MATES, RANK, SLICE), F32),
            *[pltpu.SemaphoreType.DMA(s) for s in sems],
        ],
        compiler_params=pltpu.CompilerParams(
            collective_id=0, has_side_effects=True, vmem_limit_bytes=62 << 20
        ),
        cost_estimate=pl.CostEstimate(flops=20 << 30, bytes_accessed=16 << 20, transcendentals=0),
    )(layer_input, output_grad, slot, weights)


def per_device(layer_input, output_grad, adapter_ids, owner_map, weights, moment, second):
    slot = slot_of_rows(adapter_ids, owner_map)[None, :]
    grads = ADAPTER_SCALING * summed_grads(layer_input, output_grad, slot, weights[0])
    return adam_step(grads[None], moment, second)


def solution(mesh):
    split = Mesh(np.asarray(mesh.devices).reshape(NY, NX, NZ, NC), ("y", "x", "z", "c"))
    ep = ("x", "z", "c")
    tokens = P(("y",) + ep, None)
    state = P(ep, None, None, "y")
    return jax.shard_map(
        per_device,
        mesh=split,
        in_specs=(tokens, tokens, tokens, P(), state, state, state),
        out_specs=(state, state, state),
        check_vma=False,
    )
```

time: 493 us -> 285 us (0.58)
  waiting for transfers between devices: 410 us -> 0 us
  Pallas kernels: 0 us -> 278 us
  matrix products: 40.7 us -> 0 us
  starting transfers between devices: 19.5 us -> 0 us
  between operations: 14.1 us -> 0.65 us
    all_to_all x2 -> x0, waiting for transfers between devices: 327 us -> none  [the longest x1 178 us: per_device(): lax.all_to_all(grad_slots, 'ep', split_axis=0, concat_axis=0, tiled=True)]
    pallas_call x0 -> x1, Pallas kernels: none -> 278 us  [summed_grads(): pl.pallas_call(kernel, out_shape=jax.ShapeDtypeStruct((2, RANK, MATES * S...]
    reduce_scatter x1 -> x0, waiting for transfers between devices: 46.3 us -> none  [per_device(): lax.psum_scatter(partial_grads[None], 'grp', scatter_dimension=3, tiled=T...]
    dot_general x4 -> x0, matrix products: 40.7 us -> none  [the longest x2 15.5 us: pack_slots(): jnp.dot(matcher, values, preferred_element_type=jnp.float32)]
    all_gather x1 -> x0, waiting for transfers between devices: 36.3 us -> none  [per_device(): whole = lax.all_gather(weights, 'grp', axis=3, tiled=True)]
    all_to_all x2 -> x0, starting transfers between devices: 19.3 us -> none  [the longest x1 13.2 us: per_device(): lax.all_to_all(grad_slots, 'ep', split_axis=0, concat_axis=0, tiled=True)]
  transfers between devices with their start and end apart: 4 -> 0, of which waited for: 4 -> 0; matrix products, arithmetic and copies ran while one was open for 2% -> 0% of each run, Pallas kernels for 0% -> 0%
where the time goes in v1:
time: 285 us; the launch traced here: 284 us
  Pallas kernels  278 us (98%)
  other arithmetic  5.14 us (2%)
    pallas_call x1, Pallas kernels, summed_grads(): pl.pallas_call(kernel, out_shape=jax.ShapeDtypeStruct((2, RANK, MATES * S...  278 us

profile of v1, /device:TPU:1, one launch (start us, length us, event | category | flops | bytes accessed | tf_op | source)
XLA Modules:
  0.0 283.9 jit_solution(4338606286806034387)
XLA Ops:
  0.6 0.8 select_reduce_fusion
  1.4 0.1 convert_reduce_fusion
  1.5 0.6 multiply_add_fusion.slot_ref
  2.1 0.0 copy-start
  2.1 278.1 %shard_map.94 = f32[2,64,2048]{2,1,0:T(8,128)} custom-call(bf16[256,8192]{1,0:T(8,128)(2,1)} %x_ref.1, bf16[256,8192]{1,0:T(8,128)(2,1)} %g_ref.1, s32[1,256]{1,0:T(1,128)} %multiply_add_fusion.slot_ref, bf16[2,64,2048]{2,1,0:T(8,128)(2,1)} %bitcast.13), custom_call_target="tpu_custom_call" | custom-call | flops 21474836480 | bytes 16777216 | tf_op jit(solution)/shard_map/pallas_call | solution.py:365
  280.2 0.0 copy-done
  280.2 3.6 %add_divide_fusion = (f32[1,2,64,2048]{3,2,1,0:T(8,128)}, f32[1,2,64,2048]{3,2,1,0:T(8,128)}, f32[1,2,64,2048]{3,2,1,0:T(8,128)}) fusion(f32[2,64,2048]{2,1,0:T(8,128)} %shard_map.94, f32[1,2,64,2048]{3,2,1,0:T(8,128)S(1)} %copy-done, f32[1,2,64,2048]{3,2,1,0:T(8,128)} %param.12), kind=kLoop, calls=%fused_computation.2 | loop fusion | flops 3145728 | bytes 6291456 | tf_op jit(solution)/shard_map/div | solution.py:37
Async XLA Ops:
  2.1 278.1 %copy-start = (f32[1,2,64,2048]{3,2,1,0:T(8,128)S(1)}, f32[1,2,64,2048]{3,2,1,0:T(8,128)}, u32[]{:S(2)}) copy-start(f32[1,2,64,2048]{3,2,1,0:T(8,128)} %param.13) | copy-start | bytes 3145732

commit v2 on v1

--- a/solution.py
+++ b/solution.py
@@ -17,6 +17,7 @@
 ROWS = 256
 RANK = 64
 SLICE = 256
+QUARTER = MATES // 2
 UP, DOWN = NZ // 2, NZ // 2 - 1
 
 ADAPTER_SCALING = 2.0
@@ -60,8 +61,8 @@
 
 def kernel(
     x_ref, g_ref, slot_ref, w_ref, out_ref,
-    slots, wbuf, recv, spread, packed, part, pair, rsum, own, full, low, ring, last,
-    slot_s, slot_r, wx_s, wx_r, wz_s, wz_r, tok_s, tok_r, lc_s, lc_r, lr_s, lr_r, lg_s, lg_r,
+    slots, wbuf, recv, spread, packed, part, pair, rsum, full, low, first, ring, last,
+    slot_s, slot_r, wx_s, wx_r, wz_s, wz_r, tok_s, tok_r, lc_s, lc_r, lr_s, lr_r, lg_s, lg_r, lf_s, lf_r,
     gz_s, gz_r, gx_s, gx_r, here,
 ):
     y, x, z, c = (lax.axis_index(a) for a in ("y", "x", "z", "c"))
@@ -123,15 +124,25 @@
     def sum_copy(t, m):
         return remote(pair.at[t, m], rsum.at[t, m], lr_s.at[t, m], lr_r.at[t, m], chip(m, -1))
 
-    def low_copy(t, k):
-        return remote(own.at[t], full.at[t, k], lg_s.at[t, k], lg_r.at[t, k], peer(k))
-
-    def ring_copy(t, arm, s):
-        sign = (1 - 2 * arm) * (1 - 2 * t)
+    def low_copy(t, m):
         return remote(
-            ring.at[t, arm * (UP + 1) + s], ring.at[t, arm * (UP + 1) + s + 1],
-            gz_s.at[t, arm * UP + s], gz_r.at[t, arm * UP + s], along(-sign),
-        )
+            full.at[t, 0], full.at[t, 2 * m], lg_s.at[t, m], lg_r.at[t, m], chip(m)
+        )
+
+    def low_pass(t, m):
+        return remote(
+            full.at[t, 2 * m], full.at[t, 2 * m + 1], lf_s.at[t, m], lf_r.at[t, m], sibling
+        )
+
+    def ring_copy(t, h, arm, s):
+        sign = (1 - 2 * arm) * (1 - 2 * h)
+        sem = arm * UP + s
+        src, dst = (
+            (ring.at[t, h, sem - 1], ring.at[t, h, sem])
+            if s
+            else (first.at[t, h, arm, 0], first.at[t, h, arm, 1])
+        )
+        return remote(src, dst, gz_s.at[t, h, sem], gz_r.at[t, h, sem], along(-sign))
 
     def grad_copy(t, m):
         d = mate_at(m)
@@ -158,11 +169,26 @@
     loop(1, MATES, lambda m: weight_copy(m).start())
     loop(1, PEERS, lambda k: slot_copy(k).start())
 
-    def order(i):
-        return (i * (13 + 6 * c)) % PEERS
-
-    for t in range(2):
-        loop(1, PEERS, lambda i: token_copy(t, order(i)).start())
+    def chip_at(core, i):
+        return (i * (7 + 2 * core)) % CHIPS
+
+    def send_rows(t, lo, hi):
+        def both(i):
+            m = chip_at(c, i)
+
+            @pl.when(m > 0)
+            def _():
+                token_copy(t, 2 * m).start()
+
+            token_copy(t, 2 * m + 1).start()
+
+        loop(lo, hi, both)
+
+    def pair_at(i):
+        return 2 * chip_at(c, i), 2 * chip_at(1 - c, i) + 1
+
+    send_rows(0, 0, CHIPS)
+    send_rows(1, 0, CHIPS)
     mine = [
         pltpu.make_async_copy(w_ref.at[:, :, columns(mate)], wbuf.at[z * MATES + mate], here.at[0])
     ] + [
@@ -181,38 +207,30 @@
     weight_hop(1, 0).start()
     loop(1, PEERS, lambda k: slot_copy(k).wait_recv())
 
-    def spread_rows(t, j):
-        halves = []
+    def rows_of(i):
+        return pl.ds(pl.multiple_of(2 * CAP * i, 2 * CAP), 2 * CAP)
+
+    def take_rows(t, i):
+        ks = pair_at(i)
+
+        @pl.when(i > 0)
+        def _():
+            token_copy(t, ks[0]).wait_recv()
+
+        token_copy(t, ks[1]).wait_recv()
         for half in range(2):
             both = [
-                jnp.dot(hot(2 * j + i, half), recv[t, 2 * j + i], preferred_element_type=F32)
+                jnp.dot(hot(k, half), recv[t, k], preferred_element_type=F32)
                 .reshape(HALF, CAP, SLICE)
-                for i in range(2)
+                for k in ks
             ]
-            halves.append(jnp.concatenate(both, axis=1).astype(BF16))
-        at = pl.ds(pl.multiple_of(2 * CAP * j, 2 * CAP), 2 * CAP)
-        spread[t, 0:HALF, at, :] = halves[0]
-        spread[t, HALF:OWNERS, at, :] = halves[1]
-
-    def take_rows(t, j):
-        @pl.when(j > 0)
-        def _():
-            token_copy(t, 2 * j).wait_recv()
-
-        token_copy(t, 2 * j + 1).wait_recv()
-        spread_rows(t, j)
-
-    def low_parts(t, p):
-        packed[p] = jnp.concatenate(
-            [
-                lax.dot_general(spread[t, o], wbuf[o, t], NT, preferred_element_type=F32)
-                for o in (p, p + HALF)
-            ],
-            axis=1,
-        )
-
-    def to_rows(k):
-        lanes = packed[:, pl.ds(pl.multiple_of(CAP * k, CAP), CAP), :].reshape(HALF * CAP, 2 * RANK).T
+            spread[t, half * HALF : (half + 1) * HALF, rows_of(i), :] = jnp.concatenate(
+                both, axis=1
+            ).astype(BF16)
+
+    def to_rows(k, place):
+        at = pl.ds(pl.multiple_of(CAP * place, CAP), CAP)
+        lanes = packed[:, at, :].reshape(HALF * CAP, 2 * RANK).T
         high = lanes.astype(BF16)
         rest = (lanes - high.astype(F32)).astype(BF16)
         total = jnp.zeros((2 * RANK, ROWS), F32)
@@ -223,18 +241,27 @@
             )
         part[k] = total[:RANK] + total[RANK:]
 
-    def low_send(t):
-        loop(0, HALF, lambda p: low_parts(t, p))
-
-        def both(m):
-            to_rows(2 * m + 1)
-            pair_copy(t, m).start()
-            to_rows(2 * m)
-
-        loop(0, CHIPS, both)
-
-    def low_sum(t):
-        def over_pair(m):
+    def low_send(t, half):
+        depth = PEERS * CAP // 2
+        rows = slice(half * depth, (half + 1) * depth)
+
+        def low_parts(p):
+            packed[p, rows] = jnp.concatenate(
+                [
+                    lax.dot_general(spread[t, o, rows], wbuf[o, t], NT, preferred_element_type=F32)
+                    for o in (p, p + HALF)
+                ],
+                axis=1,
+            )
+
+        def give(i):
+            mine, theirs = pair_at(i)
+            to_rows(theirs, 2 * i + 1)
+            pair_copy(t, chip_at(1 - c, i)).start()
+            to_rows(mine, 2 * i)
+
+        def add(i):
+            m = chip_at(c, i)
             pair_copy(t, m).wait_recv()
             pair[t, m] = pair[t, m] + part[2 * m]
 
@@ -242,99 +269,125 @@
             def _():
                 sum_copy(t, m).start()
 
-        loop(0, CHIPS, over_pair)
+        loop(0, HALF, low_parts)
+        steps = half * CHIPS // 2, (half + 1) * CHIPS // 2
+        loop(*steps, give)
+        loop(*steps, add)
+
+    def low_sum(t):
         loop(1, CHIPS, lambda m: sum_copy(t, m).wait_recv())
         total = pair[t, 0]
         for m in range(1, CHIPS):
             total += rsum[t, m]
-        own[t] = total.astype(BF16)
         full[t, 0] = total.astype(BF16)
-        loop(1, PEERS, lambda k: low_copy(t, k).start())
+        low_pass(t, 0).start()
+        loop(1, CHIPS, lambda i: low_copy(t, chip_at(c, i)).start())
 
     def low_spread(t):
-        loop(1, PEERS, lambda k: low_copy(t, k).wait_recv())
-
-        def two(j):
-            both = []
-            for i in range(2):
-                k = 2 * j + i
-                both.append(
-                    jnp.concatenate(
-                        [
-                            lax.dot_general(hot(k, half), full[t, k], NT, preferred_element_type=F32)
-                            for half in range(2)
-                        ],
-                        axis=1,
-                    ).reshape(HALF, CAP, 2 * RANK)
-                )
-            at = pl.ds(pl.multiple_of(2 * CAP * j, 2 * CAP), 2 * CAP)
-            low[t, :, at, :] = jnp.concatenate(both, axis=1).astype(BF16)
-
-        loop(0, PEERS // 2, two)
-
-    def outer(t, plane, store):
+        def hand_on(i):
+            m = chip_at(c, i)
+            low_copy(t, m).wait_recv()
+            low_pass(t, m).start()
+
+        def two(i):
+            low_pass(t, chip_at(1 - c, i)).wait_recv()
+            both = [
+                jnp.concatenate(
+                    [
+                        lax.dot_general(hot(k, half), full[t, k], NT, preferred_element_type=F32)
+                        for half in range(2)
+                    ],
+                    axis=1,
+                ).reshape(HALF, CAP, 2 * RANK)
+                for k in pair_at(i)
+            ]
+            low[t, :, rows_of(i), :] = jnp.concatenate(both, axis=1).astype(BF16)
+
+        loop(1, CHIPS, hand_on)
+        loop(0, CHIPS, two)
+
+    def outer(t, plane, h, store):
         def one(i):
-            o = plane * MATES + i
+            o = plane * MATES + h * QUARTER + i
             p, half = o % HALF, o // HALF
-            lhs = low[t, p].T.astype(BF16)
+            lhs = low[t, p].T
             lhs = jnp.where(half == 0, lhs[:RANK], lhs[RANK:])
             store(i, jnp.dot(lhs, spread[1 - t, o], preferred_element_type=F32))
 
-        loop(0, MATES, one)
-
-    def ring_step(t, arm, s):
-        sign = (1 - 2 * arm) * (1 - 2 * t)
+        loop(0, QUARTER, one)
+
+    def ring_step(t, h, arm, s):
+        sign = (1 - 2 * arm) * (1 - 2 * h)
         hops = (UP, DOWN)[arm]
-        place = arm * (UP + 1) + s
+        place = arm * UP + s - 1
         if s > 0:
-            ring_copy(t, arm, s - 1).wait_recv()
+            ring_copy(t, h, arm, s - 1).wait_recv()
 
         def store(i, term):
-            ring[t, place, i] = term if s == 0 else ring[t, place, i] + term
-
-        outer(t, (z - sign * (hops - s) + NZ) % NZ, store)
-        ring_copy(t, arm, s).start()
+            if s == 0:
+                first[t, h, arm, 0, i] = term.astype(BF16)
+            elif s == 1:
+                ring[t, h, place, i] = first[t, h, arm, 1, i].astype(F32) + term
+            else:
+                ring[t, h, place, i] = ring[t, h, place, i] + term
+
+        outer(t, (z - sign * (hops - s) + NZ) % NZ, h, store)
+        ring_copy(t, h, arm, s).start()
 
     def ring_end(t):
-        ring_copy(t, 0, UP - 1).wait_recv()
-        ring_copy(t, 1, DOWN - 1).wait_recv()
-
-        def store(i, term):
-            last[t, i] = term + ring[t, UP, i] + ring[t, UP + 1 + DOWN, i]
-
-        outer(t, z, store)
-        loop(1, MATES, lambda m: grad_copy(t, m).start())
+        for h in range(2):
+            ring_copy(t, h, 0, UP - 1).wait_recv()
+            ring_copy(t, h, 1, DOWN - 1).wait_recv()
+
+            def store(i, term, h=h):
+                arrived = ring[t, h, UP - 1, i] + ring[t, h, UP + DOWN - 1, i]
+                last[t, h * QUARTER + i] = term + arrived
+
+            outer(t, z, h, store)
+
+            def give(i, h=h):
+                j = h * QUARTER + i
+                m = (j // NC - x + NX) % NX * NC + (j % NC - c + NC) % NC
+
+                @pl.when(m > 0)
+                def _():
+                    grad_copy(t, m).start()
+
+            loop(0, QUARTER, give)
         out_ref[1 - t, :, columns(mate)] = last[t, mate]
 
     def ring_both(t, s):
-        ring_step(t, 0, s)
-        if s < DOWN:
-            ring_step(t, 1, s)
+        for arm in range(2 if s < DOWN else 1):
+            for h in range(2):
+                ring_step(t, h, arm, s)
 
     for s in range(1, UP + 1):
-        loop(4 * (s - 1), 4 * s, lambda j: take_rows(0, j))
+        loop(4 * (s - 1), 4 * s, lambda i: take_rows(0, i))
         weight_wait(0, s - 1)
         if s < UP:
             weight_hop(0, s).start()
             weight_wait(1, s - 1)
         if s < DOWN:
             weight_hop(1, s).start()
-    low_send(0)
+    low_send(0, 0)
+    low_send(0, 1)
     low_sum(0)
-    loop(0, PEERS // 2, lambda j: take_rows(1, j))
+    loop(0, CHIPS // 2, lambda i: take_rows(1, i))
     loop(0, CHIPS, lambda m: pair_copy(0, m).wait_send())
-    low_send(1)
+    low_send(1, 0)
     low_spread(0)
+    loop(CHIPS // 2, CHIPS, lambda i: take_rows(1, i))
     ring_both(0, 0)
+    low_send(1, 1)
+    ring_both(0, 1)
     low_sum(1)
-    ring_both(0, 1)
+    ring_both(0, 2)
     low_spread(1)
     ring_both(1, 0)
-    ring_both(0, 2)
+    ring_both(0, 3)
     ring_both(1, 1)
-    ring_both(0, 3)
+    ring_end(0)
     ring_both(1, 2)
-    ring_end(0)
     ring_both(1, 3)
     ring_end(1)
 
@@ -342,8 +395,10 @@
         loop(1, MATES, lambda m: grad_copy(t, m).wait())
         for arm, hops in enumerate((UP, DOWN)):
             for s in range(hops):
-                ring_copy(t, arm, s).wait_send()
-        loop(1, PEERS, lambda k: low_copy(t, k).wait_send())
+                for h in range(2):
+                    ring_copy(t, h, arm, s).wait_send()
+        loop(1, CHIPS, lambda m: low_copy(t, m).wait_send())
+        loop(0, CHIPS, lambda m: low_pass(t, m).wait_send())
         loop(1, CHIPS, lambda m: sum_copy(t, m).wait_send())
         loop(1, PEERS, lambda k: token_copy(t, k).wait_send())
     loop(0, CHIPS, lambda m: pair_copy(1, m).wait_send())
@@ -359,8 +414,8 @@
     hbm = pl.BlockSpec(memory_space=pl.ANY)
     sems = [
         (PEERS,), (PEERS,), (MATES,), (MATES,), (2, UP), (2, UP), (2, PEERS), (2, PEERS),
-        (2, CHIPS), (2, CHIPS), (2, CHIPS), (2, CHIPS), (2, PEERS), (2, PEERS),
-        (2, UP + DOWN), (2, UP + DOWN), (2, MATES), (2, MATES), (3,),
+        (2, CHIPS), (2, CHIPS), (2, CHIPS), (2, CHIPS), (2, CHIPS), (2, CHIPS), (2, CHIPS), (2, CHIPS),
+        (2, 2, UP + DOWN), (2, 2, UP + DOWN), (2, MATES), (2, MATES), (3,),
     ]
     return pl.pallas_call(
         kernel,
@@ -376,10 +431,10 @@
             pltpu.VMEM((PEERS, RANK, ROWS), F32),
             pltpu.VMEM((2, CHIPS, RANK, ROWS), F32),
             pltpu.VMEM((2, CHIPS, RANK, ROWS), F32),
-            pltpu.VMEM((2, RANK, ROWS), BF16),
             pltpu.VMEM((2, PEERS, RANK, ROWS), BF16),
             pltpu.VMEM((2, HALF, PEERS * CAP, 2 * RANK), BF16),
-            pltpu.VMEM((2, UP + DOWN + 2, MATES, RANK, SLICE), F32),
+            pltpu.VMEM((2, 2, 2, 2, QUARTER, RANK, SLICE), BF16),
+            pltpu.VMEM((2, 2, UP + DOWN, QUARTER, RANK, SLICE), F32),
             pltpu.VMEM((2, MATES, RANK, SLICE), F32),
             *[pltpu.SemaphoreType.DMA(s) for s in sems],
         ],

time: 285 us -> 253 us (0.89)
  Pallas kernels: 278 us -> 247 us
    pallas_call x1, Pallas kernels: 278 us -> 247 us  [summed_grads(): pl.pallas_call(kernel, out_shape=jax.ShapeDtypeStruct((2, RANK, MATES * S...]
where the time goes in v2:
time: 253 us; the launch traced here: 252 us
  Pallas kernels  247 us (98%)
  other arithmetic  5.14 us (2%)
    pallas_call x1, Pallas kernels, summed_grads(): pl.pallas_call(kernel, out_shape=jax.ShapeDtypeStruct((2, RANK, MATES * S...  247 us

profile of v2, /device:TPU:1, one launch (start us, length us, event | category | flops | bytes accessed | tf_op | source)
XLA Modules:
  0.0 252.4 jit_solution(775266346426670548)
XLA Ops:
  0.6 0.8 select_reduce_fusion
  1.4 0.1 convert_reduce_fusion
  1.5 0.6 multiply_add_fusion.slot_ref
  2.1 0.0 copy-start
  2.1 246.6 %shard_map.94 = f32[2,64,2048]{2,1,0:T(8,128)} custom-call(bf16[256,8192]{1,0:T(8,128)(2,1)} %x_ref.1, bf16[256,8192]{1,0:T(8,128)(2,1)} %g_ref.1, s32[1,256]{1,0:T(1,128)} %multiply_add_fusion.slot_ref, bf16[2,64,2048]{2,1,0:T(8,128)(2,1)} %bitcast.13), custom_call_target="tpu_custom_call" | custom-call | flops 21474836480 | bytes 16777216 | tf_op jit(solution)/shard_map/pallas_call | solution.py:420
  248.8 0.0 copy-done
  248.8 3.6 %add_divide_fusion = (f32[1,2,64,2048]{3,2,1,0:T(8,128)}, f32[1,2,64,2048]{3,2,1,0:T(8,128)}, f32[1,2,64,2048]{3,2,1,0:T(8,128)}) fusion(f32[2,64,2048]{2,1,0:T(8,128)} %shard_map.94, f32[1,2,64,2048]{3,2,1,0:T(8,128)S(1)} %copy-done, f32[1,2,64,2048]{3,2,1,0:T(8,128)} %param.12), kind=kLoop, calls=%fused_computation.2 | loop fusion | flops 3145728 | bytes 6291456 | tf_op jit(solution)/shard_map/div | solution.py:38
Async XLA Ops:
  2.1 246.6 %copy-start = (f32[1,2,64,2048]{3,2,1,0:T(8,128)S(1)}, f32[1,2,64,2048]{3,2,1,0:T(8,128)}, u32[]{:S(2)}) copy-start(f32[1,2,64,2048]{3,2,1,0:T(8,128)} %param.13) | copy-start | bytes 3145732

commit v3 on v2

--- a/solution.py
+++ b/solution.py
@@ -17,6 +17,10 @@
 ROWS = 256
 RANK = 64
 SLICE = 256
+HOPS = 5, 9, 12
+SUM_AT, SPREAD_AT = 5, 12
+WINDOW = 8
+EXTRA = 3
 QUARTER = MATES // 2
 UP, DOWN = NZ // 2, NZ // 2 - 1
 
@@ -172,23 +176,19 @@
     def chip_at(core, i):
         return (i * (7 + 2 * core)) % CHIPS
 
-    def send_rows(t, lo, hi):
-        def both(i):
-            m = chip_at(c, i)
-
-            @pl.when(m > 0)
-            def _():
-                token_copy(t, 2 * m).start()
-
-            token_copy(t, 2 * m + 1).start()
-
-        loop(lo, hi, both)
+    def send_step(t, i):
+        m = chip_at(c, i)
+
+        @pl.when(m > 0)
+        def _():
+            token_copy(t, 2 * m).start()
+
+        token_copy(t, 2 * m + 1).start()
 
     def pair_at(i):
         return 2 * chip_at(c, i), 2 * chip_at(1 - c, i) + 1
 
-    send_rows(0, 0, CHIPS)
-    send_rows(1, 0, CHIPS)
+    loop(0, WINDOW, lambda i: send_step(0, i))
     mine = [
         pltpu.make_async_copy(w_ref.at[:, :, columns(mate)], wbuf.at[z * MATES + mate], here.at[0])
     ] + [
@@ -361,22 +361,44 @@
             for h in range(2):
                 ring_step(t, h, arm, s)
 
+    def paced(t, lo, hi, ahead):
+        def step(i):
+            n = i + ahead
+
+            @pl.when(n < CHIPS)
+            def _():
+                send_step(t, n)
+
+            if t == 0:
+
+                @pl.when(n >= CHIPS)
+                def _():
+                    send_step(1, n - CHIPS)
+
+            take_rows(t, i)
+
+        loop(lo, hi, step)
+
+    cuts = (0, *HOPS, CHIPS)
     for s in range(1, UP + 1):
-        loop(4 * (s - 1), 4 * s, lambda i: take_rows(0, i))
+        paced(0, cuts[s - 1], cuts[s], WINDOW)
         weight_wait(0, s - 1)
         if s < UP:
             weight_hop(0, s).start()
             weight_wait(1, s - 1)
         if s < DOWN:
             weight_hop(1, s).start()
+    loop(WINDOW, WINDOW + EXTRA, lambda i: send_step(1, i))
     low_send(0, 0)
     low_send(0, 1)
+    paced(1, 0, SUM_AT, WINDOW + EXTRA)
     low_sum(0)
-    loop(0, CHIPS // 2, lambda i: take_rows(1, i))
+    paced(1, SUM_AT, CHIPS // 2, WINDOW + EXTRA)
     loop(0, CHIPS, lambda m: pair_copy(0, m).wait_send())
     low_send(1, 0)
+    paced(1, CHIPS // 2, SPREAD_AT, WINDOW + EXTRA)
     low_spread(0)
-    loop(CHIPS // 2, CHIPS, lambda i: take_rows(1, i))
+    paced(1, SPREAD_AT, CHIPS, WINDOW + EXTRA)
     ring_both(0, 0)
     low_send(1, 1)
     ring_both(0, 1)

time: 253 us -> 245 us (0.968)
  Pallas kernels: 247 us -> 238 us
    pallas_call x1, Pallas kernels: 247 us -> 238 us  [summed_grads(): pl.pallas_call(kernel, out_shape=jax.ShapeDtypeStruct((2, RANK, MATES * S...]
where the time goes in v3:
time: 245 us; the launch traced here: 244 us
  Pallas kernels  238 us (97%)
  other arithmetic  5.14 us (2%)
    pallas_call x1, Pallas kernels, summed_grads(): pl.pallas_call(kernel, out_shape=jax.ShapeDtypeStruct((2, RANK, MATES * S...  238 us

profile of v3, /device:TPU:1, one launch (start us, length us, event | category | flops | bytes accessed | tf_op | source)
XLA Modules:
  0.0 243.9 jit_solution(9390258198806957932)
XLA Ops:
  0.6 0.8 select_reduce_fusion
  1.4 0.1 convert_reduce_fusion
  1.5 0.6 multiply_add_fusion.slot_ref
  2.1 0.0 copy-start
  2.1 238.1 %shard_map.94 = f32[2,64,2048]{2,1,0:T(8,128)} custom-call(bf16[256,8192]{1,0:T(8,128)(2,1)} %x_ref.1, bf16[256,8192]{1,0:T(8,128)(2,1)} %g_ref.1, s32[1,256]{1,0:T(1,128)} %multiply_add_fusion.slot_ref, bf16[2,64,2048]{2,1,0:T(8,128)(2,1)} %bitcast.13), custom_call_target="tpu_custom_call" | custom-call | flops 21474836480 | bytes 16777216 | tf_op jit(solution)/shard_map/pallas_call | solution.py:442
  240.3 0.0 copy-done
  240.3 3.6 %add_divide_fusion = (f32[1,2,64,2048]{3,2,1,0:T(8,128)}, f32[1,2,64,2048]{3,2,1,0:T(8,128)}, f32[1,2,64,2048]{3,2,1,0:T(8,128)}) fusion(f32[2,64,2048]{2,1,0:T(8,128)} %shard_map.94, f32[1,2,64,2048]{3,2,1,0:T(8,128)S(1)} %copy-done, f32[1,2,64,2048]{3,2,1,0:T(8,128)} %param.12), kind=kLoop, calls=%fused_computation.2 | loop fusion | flops 3145728 | bytes 6291456 | tf_op jit(solution)/shard_map/div | solution.py:42
Async XLA Ops:
  2.1 238.2 %copy-start = (f32[1,2,64,2048]{3,2,1,0:T(8,128)S(1)}, f32[1,2,64,2048]{3,2,1,0:T(8,128)}, u32[]{:S(2)}) copy-start(f32[1,2,64,2048]{3,2,1,0:T(8,128)} %param.13) | copy-start | bytes 3145732
